TPU v7x, 32 devices: a whole 2x2x4 slice. The times are simulated.
32 devices in a mesh: dp: 4 (over x, core), seq: 8 (over z, y).
Axes of the slice: x: 2, y: 2, z: 4, core: 2. Of those that a mesh axis runs over, the one named last changes fastest.
Arguments:
- inputs: bfloat16 [4, 4096, 768], P('dp', 'seq'), may hold values from -6 to 6
- block_mix: bfloat16 [8, 512, 512], P('seq'), may hold values from -0.25 to 0.25
- cross_mix: bfloat16 [512, 8, 8], P('seq'), may hold values from -2 to 2
- cotangent: bfloat16 [4, 4096, 768], P('dp', 'seq'), may hold values from -0.59765625 to 0.59765625
Outputs:
- output: bfloat16 [4, 4096, 768], P('dp', 'seq')
- input_grad: bfloat16 [4, 4096, 768], P('dp', 'seq')
- block_grad: bfloat16 [8, 512, 512], P('seq')
- cross_grad: bfloat16 [512, 8, 8], P('seq')
All inputs are finite; a program needn't handle non-finite values.
Results may differ from a plain program's by a relative error of at most 0.012.
Values may be sent and summed in bfloat16 or wider, within the bound.
A program may use at most 64 MiB of HBM per device.

v0:
```python
import jax
import jax.numpy as jnp
from jax import lax
from jax.sharding import PartitionSpec as P


def local(inputs, block_mix, cross_mix, cotangent):
    h = jnp.einsum("bsr,brc->bsc", block_mix, inputs, preferred_element_type=jnp.float32).astype(
        jnp.bfloat16
    )
    gate = jax.nn.sigmoid(inputs.astype(jnp.float32))
    h_cols = lax.all_to_all(h, "seq", split_axis=1, concat_axis=0, tiled=True)
    z_cols = jnp.einsum(
        "rab,brc->arc", cross_mix, h_cols, preferred_element_type=jnp.float32
    ).astype(jnp.bfloat16)
    z = lax.all_to_all(z_cols, "seq", split_axis=0, concat_axis=1, tiled=True)
    dz = (cotangent.astype(jnp.float32) * gate).astype(jnp.bfloat16)
    dz_cols = lax.all_to_all(dz, "seq", split_axis=1, concat_axis=0, tiled=True)
    dh_cols = jnp.einsum(
        "rab,arc->brc", cross_mix, dz_cols, preferred_element_type=jnp.float32
    ).astype(jnp.bfloat16)
    cross_part = jnp.einsum("arc,brc->rab", dz_cols, h_cols, preferred_element_type=jnp.float32)
    dh = lax.all_to_all(dh_cols, "seq", split_axis=0, concat_axis=1, tiled=True)
    dv = jnp.einsum("bsr,bsc->brc", block_mix, dh, preferred_element_type=jnp.float32)
    block_part = jnp.einsum("bsc,brc->bsr", dh, inputs, preferred_element_type=jnp.float32)
    block_sum, cross_sum = (
        lax.psum(block_part.astype(jnp.bfloat16), "dp").astype(jnp.float32),
        lax.psum(cross_part.astype(jnp.bfloat16), "dp").astype(jnp.float32),
    )
    zf = z.astype(jnp.float32)
    output = (inputs.astype(jnp.float32) + zf * gate).astype(jnp.bfloat16)
    input_grad = (cotangent.astype(jnp.float32) * (1.0 + zf * gate * (1.0 - gate)) + dv).astype(
        jnp.bfloat16
    )
    return (output, input_grad, block_sum.astype(jnp.bfloat16), cross_sum.astype(jnp.bfloat16))


def solution(mesh):
    placed = (
        P("dp", "seq", None),
        P("seq", None, None),
        P("seq", None, None),
        P("dp", "seq", None),
    )
    return jax.shard_map(
        local,
        mesh=mesh,
        in_specs=placed,
        out_specs=(
            P("dp", "seq", None),
            P("dp", "seq", None),
            P("seq", None, None),
            P("seq", None, None),
        ),
        check_vma=False,
    )
```

profile of v0, /device:TPU:0, one launch (start us, length us, event | category | flops | bytes accessed | tf_op | source)
XLA Modules:
  0.0 190.0 jit_solution(17759699037681168629)
XLA Ops:
  7.2 0.0 copy-start
  7.2 1.0 copy-done
  8.2 1.7 fusion.9
  9.9 1.2 copy.73
  11.1 0.5 broadcast.12
  11.7 5.4 %reduce = bf16[512,768]{1,0:T(8,128)(2,1)S(1)} reduce(bf16[512,1,768]{2,1,0:T(2,128)(2,1)S(1)} %bitcast.39, bf16[]{:T(256)} %broadcast.12), dimensions={1}, to_apply=%bitcast.37.reduce_sub_computation | reduce | bytes 1572866
  17.1 0.0 copy-start.8
  17.1 1.1 reshape.57
  18.2 7.3 %all-to-all-start = ((bf16[8,2,24576]{2,1,0:T(2,128)(2,1)}), bf16[8,2,24576]{2,1,0:T(2,128)(2,1)S(1)}, u32[]{:S(2)}, u32[]{:S(2)}) async-start(bf16[8,2,24576]{2,1,0:T(2,128)(2,1)} %reshape.57), calls=%async_computation | async-start | bytes 1572864 | tf_op jit(solution)/shard_map/all_to_all | solution.py:12
  25.4 0.0 copy-done.8
  25.4 0.1 copy.55
  25.6 20.0 %all-to-all-done = bf16[8,2,24576]{2,1,0:T(2,128)(2,1)S(1)} async-done(((bf16[8,2,24576]{2,1,0:T(2,128)(2,1)}), bf16[8,2,24576]{2,1,0:T(2,128)(2,1)S(1)}, u32[]{:S(2)}, u32[]{:S(2)}) %all-to-all-start) | async-done | bytes 786464 | tf_op jit(solution)/shard_map/all_to_all | solution.py:12
  45.6 0.8 reshape.58
  46.4 0.1 copy.62
  46.6 0.0 copy-start.4
  46.6 0.9 copy-done.4
  47.4 0.6 fusion.7
  48.0 1.0 copy.50
  49.1 0.0 copy-start.7
  49.1 3.9 %all-to-all-start.1 = ((bf16[8,64,768]{2,1,0:T(8,128)(2,1)}), bf16[8,64,768]{2,1,0:T(8,128)(2,1)S(1)}, u32[]{:S(2)}, u32[]{:S(2)}) async-start(bf16[8,64,768]{2,1,0:T(8,128)(2,1)} %copy.50), calls=%async_computation.1 | async-start | bytes 1572864 | tf_op jit(solution)/shard_map/all_to_all | solution.py:16
  52.9 1.4 copy.46
  54.3 0.0 copy-done.7
  54.4 1.2 copy.52
  55.5 17.6 %all-to-all-done.1 = bf16[8,64,768]{2,1,0:T(8,128)(2,1)S(1)} async-done(((bf16[8,64,768]{2,1,0:T(8,128)(2,1)}), bf16[8,64,768]{2,1,0:T(8,128)(2,1)S(1)}, u32[]{:S(2)}, u32[]{:S(2)}) %all-to-all-start.1) | async-done | bytes 786464 | tf_op jit(solution)/shard_map/all_to_all | solution.py:16
  73.1 0.0 copy-start.3
  73.1 0.9 copy-done.3
  74.0 1.2 bitcast_convert_fusion
  75.2 1.6 copy.51
  76.8 3.4 %fusion.6 = (bf16[1,512,768]{1,2,0:T(8,128)(2,1)}, bf16[1,512,768]{1,2,0:T(8,128)(2,1)}) fusion(bf16[1,512,768]{1,2,0:T(8,128)(2,1)} %copy.52, bf16[1,512,768]{1,2,0:T(8,128)(2,1)S(1)} %copy.46, f32[1,512,768]{1,2,0:T(8,128)} %copy.51), kind=kLoop, calls=%fused_computation.10 | loop fusion | flops 3932160 | bytes 4718592 | tf_op jit(solution)/shard_map/convert_element_type | solution.py:17
  80.2 3.7 %copy.53 = bf16[1,512,768]{2,0,1:T(2,128)(2,1)S(1)} copy(bf16[1,512,768]{1,2,0:T(8,128)(2,1)} %get-tuple-element.20) | data formatting | bytes 1572864 | tf_op jit(solution)/shard_map/convert_element_type | solution.py:17
  84.0 6.3 %reduce.1 = bf16[512,768]{1,0:T(8,128)(2,1)} reduce(bf16[512,1,768]{2,1,0:T(2,128)(2,1)S(1)} %bitcast.40, bf16[]{:T(256)} %broadcast.12), dimensions={1}, to_apply=%bitcast.30.reduce_sub_computation | reduce | bytes 1572866
  90.3 2.2 %reshape.59 = bf16[8,2,24576]{2,1,0:T(2,128)(2,1)S(1)} reshape(bf16[512,768]{1,0:T(8,128)(2,1)} %reduce.1) | data formatting | bytes 1572864
  92.5 23.8 %all_to_all.42 = bf16[8,2,24576]{2,1,0:T(2,128)(2,1)} all-to-all(bf16[8,2,24576]{2,1,0:T(2,128)(2,1)S(1)} %reshape.59), channel_id=1, replica_groups=mesh['dp'=4,'seq'=8] {'seq'}, dimensions={0} | all-to-all | bytes 1572864 | tf_op jit(solution)/shard_map/all_to_all | solution.py:18
  116.3 4.1 %reshape.60 = bf16[512,1,768]{2,1,0:T(2,128)(2,1)S(1)} reshape(bf16[8,2,24576]{2,1,0:T(2,128)(2,1)} %all_to_all.42) | data formatting | bytes 1572864
  120.4 0.1 copy.63
  120.5 0.0 copy-start.6
  120.5 0.6 fusion.8
  121.1 0.3 copy-done.6
  121.4 0.0 copy-start.2
  121.4 1.0 copy.56
  122.5 0.0 copy-start.5
  122.5 4.3 %all-to-all-start.3 = ((bf16[8,64,768]{2,1,0:T(8,128)(2,1)}), bf16[8,64,768]{2,1,0:T(8,128)(2,1)}, u32[]{:S(2)}, u32[]{:S(2)}) async-start(bf16[8,64,768]{2,1,0:T(8,128)(2,1)} %copy.56), calls=%async_computation.3 | async-start | bytes 1572864 | tf_op jit(solution)/shard_map/all_to_all | solution.py:23
  126.8 0.0 all-reduce.2.cloned.1.call-start
  126.9 0.0 copy-done.2
  126.9 1.2 copy.59
  128.0 0.0 copy-done.5
  128.0 2.1 %convolution_convert_fusion.4 = bf16[64,8,8]{2,1,0:T(8,128)(2,1)S(1)} fusion(bf16[8,64,768]{2,1,0:T(8,128)(2,1)} %bitcast.47, bf16[8,64,768]{2,1,0:T(8,128)(2,1)S(1)} %bitcast.45), kind=kOutput, calls=%fused_computation.19 | convolution fusion | flops 6295552 | bytes 1581056 | tf_op jit(solution)/shard_map/arc,brc->rab/dot_general | solution.py:22
  130.1 12.4 %psum.15 = bf16[64,8,8]{2,1,0:T(8,128)(2,1)S(1)} all-reduce(bf16[64,8,8]{2,1,0:T(8,128)(2,1)S(1)} %convolution_convert_fusion.4), channel_id=1, replica_groups=mesh['dp'=4,'seq'=8] {'dp'}, use_global_device_ids=true, to_apply=%region_1.0 | all-reduce | flops 4096 | bytes 16384 | tf_op jit(solution)/shard_map/psum | solution.py:28
  142.5 0.0 copy-start.1
  142.5 0.7 copy.61
  143.2 3.0 %all-to-all-done.3 = bf16[8,64,768]{2,1,0:T(8,128)(2,1)} async-done(((bf16[8,64,768]{2,1,0:T(8,128)(2,1)}), bf16[8,64,768]{2,1,0:T(8,128)(2,1)}, u32[]{:S(2)}, u32[]{:S(2)}) %all-to-all-start.3) | async-done | bytes 786464 | tf_op jit(solution)/shard_map/all_to_all | solution.py:23
  146.2 2.8 %fusion.10 = bf16[1,512,512]{2,1,0:T(8,128)(2,1)} fusion(bf16[512,768]{1,0:T(8,128)(2,1)} %bitcast.6, bf16[1,512,768]{2,1,0:T(8,128)(2,1)} %param.4), kind=kOutput, calls=%fused_computation.18 | convolution fusion | flops 402915328 | bytes 2097152 | tf_op jit(solution)/shard_map/bsc,brc->bsr/dot_general | solution.py:25
  149.0 0.0 all-reduce.2.cloned.1.call-update
  149.0 0.0 copy-done.1
  149.0 3.2 %fusion.5 = bf16[1,512,768]{1,2,0:T(8,128)(2,1)} fusion(bf16[1,512,768]{1,2,0:T(8,128)(2,1)} %copy.52, bf16[512,768]{1,0:T(8,128)(2,1)} %bitcast.6, f32[1,512,768]{1,2,0:T(8,128)S(1)} %copy-done.1, bf16[1,512,512]{2,1,0:T(8,128)(2,1)S(1)} %copy-done, bf16[1,512,768]{1,2,0:T(8,128)(2,1)S(1)} %copy.46), kind=kOutput, calls=%fused_computation.9 | convolution fusion | flops 407371776 | bytes 5242880 | tf_op jit(solution)/shard_map/bsr,bsc->brc/dot_general | solution.py:24
  152.3 2.3 %copy.60 = bf16[1,512,768]{2,1,0:T(8,128)(2,1)} copy(bf16[1,512,768]{1,2,0:T(8,128)(2,1)} %fusion.5) | data formatting | bytes 1572864
  154.6 26.8 %all-reduce.2.cloned.1.call-done = bf16[1,512,512]{2,1,0:T(8,128)(2,1)} async-done(((bf16[1,512,512]{2,1,0:T(8,128)(2,1)}), bf16[1,512,512]{2,1,0:T(8,128)(2,1)}) %all-reduce.2.cloned.1.call-update) | async-done | bytes 524304 | tf_op jit(solution)/shard_map/psum | solution.py:27
  181.3 1.9 copy.75
Async XLA Ops:
  7.2 1.0 copy-start
  17.1 8.4 %copy-start.8 = (bf16[64,8,8]{0,2,1:T(8,128)(2,1)S(1)}, bf16[64,8,8]{0,2,1:T(8,128)(2,1)}, u32[]{:S(2)}) copy-start(bf16[64,8,8]{0,2,1:T(8,128)(2,1)} %param.6) | copy-start | bytes 24580
  18.2 27.5 %all-to-all-start = ((bf16[8,2,24576]{2,1,0:T(2,128)(2,1)}), bf16[8,2,24576]{2,1,0:T(2,128)(2,1)S(1)}, u32[]{:S(2)}, u32[]{:S(2)}) async-start(bf16[8,2,24576]{2,1,0:T(2,128)(2,1)} %reshape.57), calls=%async_computation | async-start | bytes 1572864 | tf_op jit(solution)/shard_map/all_to_all | solution.py:12
  46.6 0.9 copy-start.4
  49.1 5.3 %copy-start.7 = (bf16[1,512,768]{2,1,0:T(8,128)(2,1)S(1)}, bf16[1,512,768]{2,1,0:T(8,128)(2,1)}, u32[]{:S(2)}) copy-start(bf16[1,512,768]{2,1,0:T(8,128)(2,1)} %param.7) | copy-start | bytes 2359300
  49.1 24.0 %all-to-all-start.1 = ((bf16[8,64,768]{2,1,0:T(8,128)(2,1)}), bf16[8,64,768]{2,1,0:T(8,128)(2,1)S(1)}, u32[]{:S(2)}, u32[]{:S(2)}) async-start(bf16[8,64,768]{2,1,0:T(8,128)(2,1)} %copy.50), calls=%async_computation.1 | async-start | bytes 1572864 | tf_op jit(solution)/shard_map/all_to_all | solution.py:16
  73.1 0.9 copy-start.3
  120.5 0.9 copy-start.6
  121.4 5.4 %copy-start.2 = (bf16[1,512,768]{1,2,0:T(8,128)(2,1)S(1)}, bf16[1,512,768]{1,2,0:T(8,128)(2,1)}, u32[]{:S(2)}) copy-start(bf16[1,512,768]{1,2,0:T(8,128)(2,1)} %get-tuple-element.21) | copy-start | bytes 2359300
  122.5 5.6 %copy-start.5 = (bf16[1,512,768]{2,1,0:T(8,128)(2,1)S(1)}, bf16[1,512,768]{2,1,0:T(8,128)(2,1)}, u32[]{:S(2)}) copy-start(bf16[1,512,768]{2,1,0:T(8,128)(2,1)} %copy-done.4) | copy-start | bytes 2359300
  122.5 23.8 %all-to-all-start.3 = ((bf16[8,64,768]{2,1,0:T(8,128)(2,1)}), bf16[8,64,768]{2,1,0:T(8,128)(2,1)}, u32[]{:S(2)}, u32[]{:S(2)}) async-start(bf16[8,64,768]{2,1,0:T(8,128)(2,1)} %copy.56), calls=%async_computation.3 | async-start | bytes 1572864 | tf_op jit(solution)/shard_map/all_to_all | solution.py:23
  126.8 54.5 %all-reduce.2.cloned.1.call-start = ((), (), s32[]{:S(2)}) async-start(), calls=%async_computation.4 | async-start | bytes 1048576 | tf_op jit(solution)/shard_map/psum | solution.py:27
  142.5 6.5 %copy-start.1 = (f32[1,512,768]{1,2,0:T(8,128)S(1)}, f32[1,512,768]{1,2,0:T(8,128)}, u32[]{:S(2)}) copy-start(f32[1,512,768]{1,2,0:T(8,128)} %copy.51) | copy-start | bytes 4718596
Sparse Core Ops, SparseCore 0:
  149.2 32.1 all-reduce.1
where the time goes:
time: 191 us; the launch traced here: 190 us
  waiting for transfers between devices  67.4 us (35%)
  blocking collectives  36.1 us (19%)
  local copies, waits for them, and re-layouts  29.5 us (15%)
  other arithmetic  16.4 us (9%)
  starting transfers between devices  15.5 us (8%)
  between operations  14.2 us (7%)
  matrix products  10.9 us (6%)
    psum x1, waiting for transfers between devices, local(): lax.psum(block_part.astype(jnp.bfloat16), 'dp').astype(jnp.float32)  26.8 us
    all_to_all x1, blocking collectives, local(): dz_cols = lax.all_to_all(dz, 'seq', split_axis=1, concat_axis=0, tiled=True)  23.8 us
    unnamed x32, local copies, waits for them, and re-layouts  20.9 us
    all_to_all x1, waiting for transfers between devices, local(): h_cols = lax.all_to_all(h, 'seq', split_axis=1, concat_axis=0, tiled=True)  20 us
    all_to_all x1, waiting for transfers between devices, local(): z = lax.all_to_all(z_cols, 'seq', split_axis=0, concat_axis=1, tiled=True)  17.6 us
    psum x1, blocking collectives, local(): lax.psum(cross_part.astype(jnp.bfloat16), 'dp').astype(jnp.float32)  12.4 us
    unnamed x2, other arithmetic  11.7 us
    all_to_all x1, starting transfers between devices, local(): h_cols = lax.all_to_all(h, 'seq', split_axis=1, concat_axis=0, tiled=True)  7.28 us
  transfers between devices with their start and end apart: 4, of which 4 were waited for; matrix products, arithmetic and copies ran while one was open for 6% of the time, Pallas kernels for 0%

commit v1 on v0

--- a/solution.py
+++ b/solution.py
@@ -24,7 +24,7 @@
     dv = jnp.einsum("bsr,bsc->brc", block_mix, dh, preferred_element_type=jnp.float32)
     block_part = jnp.einsum("bsc,brc->bsr", dh, inputs, preferred_element_type=jnp.float32)
     block_sum, cross_sum = (
-        lax.psum(block_part.astype(jnp.bfloat16), "dp").astype(jnp.float32),
+        jnp.sum(lax.all_gather(block_part.astype(jnp.bfloat16), "dp"), axis=0).astype(jnp.float32),
         lax.psum(cross_part.astype(jnp.bfloat16), "dp").astype(jnp.float32),
     )
     zf = z.astype(jnp.float32)

time: 191 us -> 181 us (0.948)
  waiting for transfers between devices: 67.4 us -> 37.6 us
  blocking collectives: 36.1 us -> 60.4 us
  starting transfers between devices: 15.5 us -> 11.2 us
  other arithmetic: 16.4 us -> 19.3 us
  local copies, waits for them, and re-layouts: 29.5 us -> 27.4 us
    psum x1 -> x0, waiting for transfers between devices: 26.8 us -> none  [local(): lax.psum(block_part.astype(jnp.bfloat16), 'dp').astype(jnp.float32)]
    all_to_all x0 -> x1, blocking collectives: none -> 23.2 us  [local(): dh = lax.all_to_all(dh_cols, 'seq', split_axis=0, concat_axis=1, tiled=True)]
    all_to_all x1 -> x0, starting transfers between devices: 4.34 us -> none  [local(): dh = lax.all_to_all(dh_cols, 'seq', split_axis=0, concat_axis=1, tiled=True)]
    all_to_all x1 -> x0, waiting for transfers between devices: 3.01 us -> none  [local(): dh = lax.all_to_all(dh_cols, 'seq', split_axis=0, concat_axis=1, tiled=True)]
    reduce_sum x0 -> x1, other arithmetic: none -> 2.85 us  [local(): jnp.sum(lax.all_gather(block_part.astype(jnp.bfloat16), 'dp'), axis=0)]
    unnamed x32 -> x33, local copies, waits for them, and re-layouts: 20.9 us -> 19.7 us
  transfers between devices with their start and end apart: 4 -> 3, of which waited for: 4 -> 2; matrix products, arithmetic and copies ran while one was open for 6% -> 7% of each run, Pallas kernels for 0% -> 0%
where the time goes in v1:
time: 181 us; the launch traced here: 180 us
  blocking collectives  60.4 us (33%)
  waiting for transfers between devices  37.6 us (21%)
  local copies, waits for them, and re-layouts  27.4 us (15%)
  other arithmetic  19.3 us (11%)
  between operations  14.2 us (8%)
  starting transfers between devices  11.2 us (6%)
  matrix products  9.93 us (5%)
    all_to_all x1, blocking collectives, local(): dz_cols = lax.all_to_all(dz, 'seq', split_axis=1, concat_axis=0, tiled=True)  23.7 us
    all_to_all x1, blocking collectives, local(): dh = lax.all_to_all(dh_cols, 'seq', split_axis=0, concat_axis=1, tiled=True)  23.2 us
    all_to_all x1, waiting for transfers between devices, local(): h_cols = lax.all_to_all(h, 'seq', split_axis=1, concat_axis=0, tiled=True)  20 us
    unnamed x33, local copies, waits for them, and re-layouts  19.7 us
    all_to_all x1, waiting for transfers between devices, local(): z = lax.all_to_all(z_cols, 'seq', split_axis=0, concat_axis=1, tiled=True)  17.6 us
    psum x1, blocking collectives, local(): lax.psum(cross_part.astype(jnp.bfloat16), 'dp').astype(jnp.float32)  13.4 us
    unnamed x2, other arithmetic  11.7 us
    all_to_all x1, starting transfers between devices, local(): h_cols = lax.all_to_all(h, 'seq', split_axis=1, concat_axis=0, tiled=True)  7.28 us
  transfers between devices with their start and end apart: 3, of which 2 were waited for; matrix products, arithmetic and copies ran while one was open for 7% of the time, Pallas kernels for 0%

profile of v1, /device:TPU:0, one launch (start us, length us, event | category | flops | bytes accessed | tf_op | source)
XLA Modules:
  0.0 180.0 jit_solution(18068911477165368625)
XLA Ops:
  7.2 0.0 copy-start
  7.2 1.0 copy-done
  8.2 1.7 fusion.9
  9.9 1.2 copy.73
  11.1 0.5 broadcast.12
  11.7 5.4 %reduce.3 = bf16[512,768]{1,0:T(8,128)(2,1)S(1)} reduce(bf16[512,1,768]{2,1,0:T(2,128)(2,1)S(1)} %bitcast.39, bf16[]{:T(256)} %broadcast.12), dimensions={1}, to_apply=%bitcast.37.reduce_sub_computation | reduce | bytes 1572866
  17.1 0.0 copy-start.9
  17.1 1.1 reshape.61
  18.2 7.3 %all-to-all-start = ((bf16[8,2,24576]{2,1,0:T(2,128)(2,1)}), bf16[8,2,24576]{2,1,0:T(2,128)(2,1)S(1)}, u32[]{:S(2)}, u32[]{:S(2)}) async-start(bf16[8,2,24576]{2,1,0:T(2,128)(2,1)} %reshape.61), calls=%async_computation | async-start | bytes 1572864 | tf_op jit(solution)/shard_map/all_to_all | solution.py:12
  25.4 0.0 copy-done.9
  25.4 0.1 copy.55
  25.6 20.0 %all-to-all-done = bf16[8,2,24576]{2,1,0:T(2,128)(2,1)S(1)} async-done(((bf16[8,2,24576]{2,1,0:T(2,128)(2,1)}), bf16[8,2,24576]{2,1,0:T(2,128)(2,1)S(1)}, u32[]{:S(2)}, u32[]{:S(2)}) %all-to-all-start) | async-done | bytes 786464 | tf_op jit(solution)/shard_map/all_to_all | solution.py:12
  45.6 0.8 reshape.62
  46.4 0.1 copy.62
  46.6 0.0 copy-start.4
  46.6 0.9 copy-done.4
  47.5 0.6 fusion.7
  48.0 1.0 copy.50
  49.1 0.0 copy-start.6
  49.1 3.7 %all-to-all-start.1 = ((bf16[8,64,768]{2,1,0:T(8,128)(2,1)}), bf16[8,64,768]{2,1,0:T(8,128)(2,1)S(1)}, u32[]{:S(2)}, u32[]{:S(2)}) async-start(bf16[8,64,768]{2,1,0:T(8,128)(2,1)} %copy.50), calls=%async_computation.1 | async-start | bytes 1572864 | tf_op jit(solution)/shard_map/all_to_all | solution.py:16
  52.8 0.2 all-gather.3.cloned.1.call-start
  53.0 1.4 copy.46
  54.4 0.0 copy-done.6
  54.4 1.2 copy.52
  55.6 17.6 %all-to-all-done.1 = bf16[8,64,768]{2,1,0:T(8,128)(2,1)S(1)} async-done(((bf16[8,64,768]{2,1,0:T(8,128)(2,1)}), bf16[8,64,768]{2,1,0:T(8,128)(2,1)S(1)}, u32[]{:S(2)}, u32[]{:S(2)}) %all-to-all-start.1) | async-done | bytes 786464 | tf_op jit(solution)/shard_map/all_to_all | solution.py:16
  73.1 0.0 copy-start.3
  73.1 0.9 copy-done.3
  74.0 1.2 bitcast_convert_fusion
  75.3 1.6 copy.51
  76.9 3.4 %fusion.6 = (bf16[1,512,768]{1,2,0:T(8,128)(2,1)}, bf16[1,512,768]{1,2,0:T(8,128)(2,1)}) fusion(bf16[1,512,768]{1,2,0:T(8,128)(2,1)} %copy.52, bf16[1,512,768]{1,2,0:T(8,128)(2,1)S(1)} %copy.46, f32[1,512,768]{1,2,0:T(8,128)} %copy.51), kind=kLoop, calls=%fused_computation.10 | loop fusion | flops 3932160 | bytes 4718592 | tf_op jit(solution)/shard_map/convert_element_type | solution.py:17
  80.3 3.7 %copy.53 = bf16[1,512,768]{2,0,1:T(2,128)(2,1)S(1)} copy(bf16[1,512,768]{1,2,0:T(8,128)(2,1)} %get-tuple-element.20) | data formatting | bytes 1572864 | tf_op jit(solution)/shard_map/convert_element_type | solution.py:17
  84.1 6.3 %reduce.4 = bf16[512,768]{1,0:T(8,128)(2,1)} reduce(bf16[512,1,768]{2,1,0:T(2,128)(2,1)S(1)} %bitcast.40, bf16[]{:T(256)} %broadcast.12), dimensions={1}, to_apply=%bitcast.30.reduce_sub_computation | reduce | bytes 1572866
  90.4 2.2 %reshape.63 = bf16[8,2,24576]{2,1,0:T(2,128)(2,1)S(1)} reshape(bf16[512,768]{1,0:T(8,128)(2,1)} %reduce.4) | data formatting | bytes 1572864
  92.6 23.7 %all_to_all.42 = bf16[8,2,24576]{2,1,0:T(2,128)(2,1)} all-to-all(bf16[8,2,24576]{2,1,0:T(2,128)(2,1)S(1)} %reshape.63), channel_id=1, replica_groups=mesh['dp'=4,'seq'=8] {'seq'}, dimensions={0} | all-to-all | bytes 1572864 | tf_op jit(solution)/shard_map/all_to_all | solution.py:18
  116.4 4.1 %reshape.64 = bf16[512,1,768]{2,1,0:T(2,128)(2,1)S(1)} reshape(bf16[8,2,24576]{2,1,0:T(2,128)(2,1)} %all_to_all.42) | data formatting | bytes 1572864
  120.5 0.1 copy.63
  120.6 0.0 copy-start.5
  120.6 0.6 fusion.8
  121.2 0.0 copy-start.7
  121.2 0.1 copy.56
  121.3 0.2 copy-done.5
  121.5 23.2 %all_to_all.43 = bf16[8,64,768]{2,1,0:T(8,128)(2,1)S(1)} all-to-all(bf16[8,64,768]{2,1,0:T(8,128)(2,1)S(1)} %copy.56), channel_id=1, replica_groups=mesh['dp'=4,'seq'=8] {'seq'}, dimensions={0} | all-to-all | bytes 1572864 | tf_op jit(solution)/shard_map/all_to_all | solution.py:23
  144.7 0.0 copy-start.8
  144.7 0.0 copy-start.2
  144.7 0.9 copy-done.8
  145.6 0.0 copy-done.7
  145.6 1.4 convolution_convert_fusion.3
  147.0 0.0 all-gather.3.cloned.1.call-update
  147.0 0.0 copy-done.2
  147.0 1.2 copy.59
  148.2 0.0 copy-start.1
  148.2 2.4 %convolution_convert_fusion.4 = bf16[64,8,8]{2,1,0:T(8,128)(2,1)S(1)} fusion(bf16[8,64,768]{2,1,0:T(8,128)(2,1)} %bitcast.47, bf16[8,64,768]{2,1,0:T(8,128)(2,1)} %bitcast.45), kind=kOutput, calls=%fused_computation.18 | convolution fusion | flops 6295552 | bytes 1581056 | tf_op jit(solution)/shard_map/arc,brc->rab/dot_general | solution.py:22
  150.6 13.4 %psum.7 = bf16[64,8,8]{2,1,0:T(8,128)(2,1)S(1)} all-reduce(bf16[64,8,8]{2,1,0:T(8,128)(2,1)S(1)} %convolution_convert_fusion.4), channel_id=1, replica_groups=mesh['dp'=4,'seq'=8] {'dp'}, use_global_device_ids=true, to_apply=%region_1.0 | all-reduce | flops 4096 | bytes 16384 | tf_op jit(solution)/shard_map/psum | solution.py:28
  164.0 0.7 copy.61
  164.7 0.0 copy-done.1
  164.7 3.3 %fusion.5 = bf16[1,512,768]{1,2,0:T(8,128)(2,1)} fusion(bf16[1,512,768]{1,2,0:T(8,128)(2,1)} %copy.52, bf16[512,768]{1,0:T(8,128)(2,1)} %bitcast.50, f32[1,512,768]{1,2,0:T(8,128)S(1)} %copy-done.1, bf16[1,512,512]{2,1,0:T(8,128)(2,1)S(1)} %copy-done, bf16[1,512,768]{1,2,0:T(8,128)(2,1)S(1)} %copy.46), kind=kOutput, calls=%fused_computation.9 | convolution fusion | flops 407371776 | bytes 5242880 | tf_op jit(solution)/shard_map/bsr,bsc->brc/dot_general | solution.py:24
  168.0 2.3 %copy.60 = bf16[1,512,768]{2,1,0:T(8,128)(2,1)} copy(bf16[1,512,768]{1,2,0:T(8,128)(2,1)} %fusion.5) | data formatting | bytes 1572864
  170.3 0.0 all-gather.3.cloned.1.call-done
  170.3 2.9 %reduce.2 = bf16[512,512]{1,0:T(8,128)(2,1)} reduce(bf16[4,512,512]{2,1,0:T(8,128)(2,1)} %bitcast.48, bf16[]{:T(256)} %constant.4.clone.1), dimensions={0}, to_apply=%region_0.0 | reduce | flops 786432 | bytes 2621442 | tf_op jit(solution)/shard_map/reduce_sum | solution.py:27
Async XLA Ops:
  7.2 1.0 copy-start
  17.1 8.4 %copy-start.9 = (bf16[64,8,8]{0,2,1:T(8,128)(2,1)S(1)}, bf16[64,8,8]{0,2,1:T(8,128)(2,1)}, u32[]{:S(2)}) copy-start(bf16[64,8,8]{0,2,1:T(8,128)(2,1)} %param.6) | copy-start | bytes 24580
  18.2 27.5 %all-to-all-start = ((bf16[8,2,24576]{2,1,0:T(2,128)(2,1)}), bf16[8,2,24576]{2,1,0:T(2,128)(2,1)S(1)}, u32[]{:S(2)}, u32[]{:S(2)}) async-start(bf16[8,2,24576]{2,1,0:T(2,128)(2,1)} %reshape.61), calls=%async_computation | async-start | bytes 1572864 | tf_op jit(solution)/shard_map/all_to_all | solution.py:12
  46.6 0.9 copy-start.4
  49.1 5.3 %copy-start.6 = (bf16[1,512,768]{2,1,0:T(8,128)(2,1)S(1)}, bf16[1,512,768]{2,1,0:T(8,128)(2,1)}, u32[]{:S(2)}) copy-start(bf16[1,512,768]{2,1,0:T(8,128)(2,1)} %param.7) | copy-start | bytes 2359300
  49.1 24.1 %all-to-all-start.1 = ((bf16[8,64,768]{2,1,0:T(8,128)(2,1)}), bf16[8,64,768]{2,1,0:T(8,128)(2,1)S(1)}, u32[]{:S(2)}, u32[]{:S(2)}) async-start(bf16[8,64,768]{2,1,0:T(8,128)(2,1)} %copy.50), calls=%async_computation.1 | async-start | bytes 1572864 | tf_op jit(solution)/shard_map/all_to_all | solution.py:16
  52.8 117.5 %all-gather.3.cloned.1.call-start = ((), (), s32[]{:S(2)}) async-start(), calls=%async_computation.4 | async-start | bytes 2621440 | tf_op jit(solution)/shard_map/all_gather | solution.py:27
  73.1 0.9 copy-start.3
  120.6 0.9 copy-start.5
  121.2 24.4 %copy-start.7 = (bf16[1,512,768]{2,1,0:T(8,128)(2,1)S(1)}, bf16[1,512,768]{2,1,0:T(8,128)(2,1)}, u32[]{:S(2)}) copy-start(bf16[1,512,768]{2,1,0:T(8,128)(2,1)} %param.4) | copy-start | bytes 2359300
  144.7 0.9 copy-start.8
  144.7 2.3 %copy-start.2 = (bf16[1,512,768]{1,2,0:T(8,128)(2,1)S(1)}, bf16[1,512,768]{1,2,0:T(8,128)(2,1)}, u32[]{:S(2)}) copy-start(bf16[1,512,768]{1,2,0:T(8,128)(2,1)} %get-tuple-element.21) | copy-start | bytes 2359300
  148.2 16.6 %copy-start.1 = (f32[1,512,768]{1,2,0:T(8,128)S(1)}, f32[1,512,768]{1,2,0:T(8,128)}, u32[]{:S(2)}) copy-start(f32[1,512,768]{1,2,0:T(8,128)} %copy.51) | copy-start | bytes 4718596
Sparse Core Ops, SparseCore 0:
  147.1 22.9 all-gather.2
